TPU v7x, 32 devices: a whole 2x2x4 slice. The times are simulated.
32 devices in a mesh: groups: 2 (over y), state: 4 (over z), member: 4 (over x, core).
Axes of the slice: x: 2, y: 2, z: 4, core: 2. Of those that a mesh axis runs over, the one named last changes fastest.
Arguments:
- ensemble: bfloat16 [256, 65536], P('member', ('groups', 'state')), parts along dimension 1, may hold values from -6 to 6
- obs_value: float32 [6, 1024], P(None, ('groups', 'state', 'member')), parts along dimension 1, may hold values from -6 to 6
- obs_var: float32 [6, 1024], P(None, ('groups', 'state', 'member')), parts along dimension 1, may hold values from 0.3 to 4
- obs_site: int32 [6, 1024], P(None, ('groups', 'state', 'member')), parts along dimension 1, may hold values from 0 to 2047
- loc_pattern: int32 [6, 32, 8], P(None, ('groups', 'state', 'member')), parts along dimension 1, may hold values 0 or 1
Outputs:
- posterior: bfloat16 [256, 65536], P('member', ('groups', 'state')), parts along dimension 1
There are 2 independent parts, one for each index of `groups`. A program takes and returns all parts, laid end to end along the dimension named above; each array names one. Nothing has to cross between parts.
All inputs are finite; a program needn't handle non-finite values. No bound on the sum of `loc_pattern` on one device may be relied on, other than what follows from the above.
Results may differ from a plain program's by a relative error of at most 0.023.
Values may be sent and summed in bfloat16 or wider, within the bound.
A program may use at most 64 MiB of HBM per device.

v0:
```python
import jax
import jax.numpy as jnp
from jax import lax
from jax.sharding import PartitionSpec as P

BATCHES = 6


EPS = 1e-05


def panel_from_prior(prior, ovar, oval):
    members = prior.shape[1]
    ymean = jnp.mean(prior, axis=1, keepdims=True)
    yanom = prior - ymean
    spread = jnp.sum(yanom * yanom, axis=1) / (members - 1.0)
    post_mean = (ymean[:, 0] * ovar + oval * spread) / (ovar + spread)
    shrink = jnp.sqrt(ovar / (ovar + spread))
    incr = (post_mean[:, None] + shrink[:, None] * yanom - prior).astype(jnp.bfloat16)
    gain = 1.0 / ((members - 1.0) * (spread + EPS))
    return (yanom.astype(jnp.bfloat16), incr, gain)


def apply_rows(total, xanom, yanom_b, incr, gain, wrow):
    cov = jnp.dot(yanom_b, xanom, preferred_element_type=jnp.float32)
    weights = (cov * (gain * wrow)[:, None]).astype(jnp.bfloat16)
    return total + lax.dot_general(
        incr, weights, (((0,), (0,)), ((), ())), preferred_element_type=jnp.float32
    )


def per_device(ensemble, obs_value, obs_var, obs_site, loc_pattern):
    gathered = lax.all_to_all(ensemble, "member", split_axis=1, concat_axis=0, tiled=True)
    state = gathered.astype(jnp.float32)
    members = gathered.shape[0]
    own_obs = obs_site.shape[1]
    nblocks = loc_pattern.shape[1] * lax.axis_size(("state", "member"))
    total_obs = own_obs * nblocks
    ntiles = loc_pattern.shape[2]
    obs_tile = total_obs // ntiles
    own_cols = jnp.take(gathered, obs_site.reshape(-1), axis=1)
    all_cols, all_loc = (
        lax.all_gather(own_cols, ("state", "member"), axis=1, tiled=True),
        lax.all_gather(loc_pattern.astype(jnp.bfloat16), ("state", "member"), axis=1, tiled=True),
    )
    all_vals, all_vars = (
        lax.all_gather(obs_value, ("state", "member"), axis=1, tiled=True),
        lax.all_gather(obs_var, ("state", "member"), axis=1, tiled=True),
    )
    columns = all_cols.astype(jnp.float32).reshape(members, nblocks, BATCHES, own_obs)
    columns = columns.transpose(2, 0, 1, 3).reshape(BATCHES, members, total_obs)
    col_block = jnp.arange(total_obs, dtype=jnp.int32) // own_obs
    block_onehot = (col_block[:, None] == jnp.arange(nblocks, dtype=jnp.int32)[None, :]).astype(
        jnp.float32
    )
    obs_tiles = jnp.arange(total_obs, dtype=jnp.int32) // obs_tile
    tile_onehot = (obs_tiles[:, None] == jnp.arange(ntiles, dtype=jnp.int32)[None, :]).astype(
        jnp.float32
    )
    for batch in range(BATCHES):
        prior = columns[batch].T
        yanom_b, incr, gain = panel_from_prior(prior, all_vars[batch], all_vals[batch])
        wrow = jnp.repeat(loc_pattern[batch, 0].astype(jnp.float32), obs_tile)
        xanom = (state - jnp.mean(state, axis=0, keepdims=True)).astype(jnp.bfloat16)
        state = apply_rows(state, xanom, yanom_b, incr, gain, wrow)
        if batch + 1 < BATCHES:
            later = columns[batch + 1 :].transpose(1, 0, 2).reshape(members, -1)
            col_anom = (later - jnp.mean(later, axis=0, keepdims=True)).astype(jnp.bfloat16)
            loc_now = all_loc[batch].astype(jnp.float32)
            col_loc = jnp.dot(
                jnp.dot(block_onehot, loc_now, precision=lax.Precision.HIGHEST),
                tile_onehot.T,
                precision=lax.Precision.HIGHEST,
            )
            wmat = jnp.tile(col_loc.T, (1, BATCHES - batch - 1))
            cov = jnp.dot(yanom_b, col_anom, preferred_element_type=jnp.float32)
            weights = (cov * gain[:, None] * wmat).astype(jnp.bfloat16)
            later = later + lax.dot_general(
                incr, weights, (((0,), (0,)), ((), ())), preferred_element_type=jnp.float32
            )
            later = later.reshape(members, BATCHES - batch - 1, total_obs).transpose(1, 0, 2)
            columns = jnp.concatenate([columns[: batch + 1], later], axis=0)
    return lax.all_to_all(
        state.astype(jnp.bfloat16), "member", split_axis=0, concat_axis=1, tiled=True
    )


def solution(mesh):
    in_specs = (
        P("member", ("groups", "state")),
        P(None, ("groups", "state", "member")),
        P(None, ("groups", "state", "member")),
        P(None, ("groups", "state", "member")),
        P(None, ("groups", "state", "member"), None),
    )
    out_specs = P("member", ("groups", "state"))
    return jax.shard_map(
        per_device, mesh=mesh, in_specs=in_specs, out_specs=out_specs, check_vma=False
    )
```

profile of v0, /device:TPU:0, one launch (start us, length us, event | category | flops | bytes accessed | tf_op | source)
XLA Modules:
  0.0 232.1 jit_solution(15802988696986075205)
XLA Ops:
  6.5 2.4 %copy.75 = bf16[8,4,8,2048]{3,2,0,1:T(8,128)(2,1)} copy(bf16[8,4,8,2048]{3,2,1,0:T(8,128)(2,1)} %bitcast.292) | data formatting | bytes 2097152 | tf_op jit(solution)/shard_map/all_to_all | solution.py:33
  8.9 4.2 %all-to-all-start = ((bf16[64,4,2048]{2,0,1:T(8,128)(2,1)}), bf16[64,4,2048]{2,0,1:T(8,128)(2,1)S(1)}, u32[]{:S(2)}, u32[]{:S(2)}) async-start(bf16[64,4,2048]{2,0,1:T(8,128)(2,1)} %bitcast.251), calls=%async_computation | async-start | bytes 2097152 | tf_op jit(solution)/shard_map/all_to_all | solution.py:33
  13.1 29.0 %all-gather = f32[16,32,6]{1,2,0:T(8,128)S(1)} all-gather(f32[1,32,6]{1,2,0:T(8,128)S(1)} %bitcast.310), channel_id=1, replica_groups=mesh['groups'=2,'state'=4,'member'=4] {'state','member'}, dimensions={0}, use_global_device_ids=true | all-gather | bytes 13056 | tf_op jit(solution)/shard_map/all_gather | solution.py:48
  42.2 17.5 %all_gather.15 = bf16[6,16,8]{2,0,1:T(8,128)(2,1)S(1)} all-gather(bf16[6,1,8]{2,0,1:T(8,128)(2,1)S(1)} %copy_convert_fusion), channel_id=1, replica_groups=mesh['groups'=2,'state'=4,'member'=4] {'state','member'}, dimensions={1}, use_global_device_ids=true | all-gather | bytes 1632 | tf_op jit(solution)/shard_map/all_gather | solution.py:44
  59.7 18.9 %all-gather.1 = f32[16,32,6]{1,2,0:T(8,128)S(1)} all-gather(f32[1,32,6]{1,2,0:T(8,128)S(1)} %bitcast.311), channel_id=1, replica_groups=mesh['groups'=2,'state'=4,'member'=4] {'state','member'}, dimensions={0}, use_global_device_ids=true | all-gather | bytes 13056 | tf_op jit(solution)/shard_map/all_gather | solution.py:47
  79.8 1.0 gather_fusion
  80.8 0.7 select_bitcast_fusion
  81.8 0.7 fusion.60
  82.6 3.0 %tile.16 = f32[512,5,512]{0,2,1:T(8,128)} broadcast(f32[512,512]{0,1:T(8,128)S(1)} %fusion.60), dimensions={0,2} | broadcast | bytes 6291456 | tf_op jit(solution)/shard_map/tile | solution.py:75
  85.6 6.0 %copy.37 = f32[512,2560]{1,0:T(8,128)} copy(f32[512,2560]{0,1:T(8,128)} %bitcast.272) | data formatting | bytes 10485760 | tf_op jit(solution)/shard_map/tile | solution.py:75
  92.0 0.6 fusion.59
  92.7 0.7 tile.18
  93.4 4.0 %copy.67 = f32[64,8,4,512]{3,1,2,0:T(8,128)} copy(f32[64,8,4,512]{3,2,1,0:T(4,128)S(1)} %bitcast.273) | data formatting | bytes 8388608
  97.8 0.7 fusion.58
  99.0 2.3 %copy.45 = f32[512,1536]{1,0:T(8,128)} copy(f32[512,1536]{0,1:T(8,128)S(1)} %bitcast.282) | data formatting | bytes 6291456 | tf_op jit(solution)/shard_map/tile | solution.py:75
  101.8 0.6 fusion.57
  102.4 0.7 tile.42
  103.1 1.8 copy.69
  105.8 13.0 %all-gather.4.cloned.1.call-done = bf16[256,3072]{0,1:T(8,128)(2,1)} async-done(((bf16[256,192]{0,1:T(8,128)(2,1)}), bf16[256,3072]{0,1:T(8,128)(2,1)}) %all-gather.4.cloned.1.call-update) | async-done | bytes 1572880 | tf_op jit(solution)/shard_map/all_gather | solution.py:43
  118.7 1.8 copy_bitcast_fusion
  121.5 2.1 copy.38
  123.9 1.0 fusion.38
  124.9 6.8 %convolution_add_fusion = f32[256,2560]{1,0:T(8,128)} fusion(f32[256,2560]{1,0:T(8,128)} %copy.38, bf16[512,256]{1,0:T(8,128)(2,1)} %get-tuple-element.10, f32[512,2560]{1,0:T(8,128)} %copy.37, bf16[512,256]{1,0:T(8,128)(2,1)S(1)} %get-tuple-element.9, f32[512]{0:T(512)S(1)} %get-tuple-element.63, f32[256,2560]{0,1:T(8,128)S(1)} %bitcast.253, f32[2560]{0:T(1024)S(1)} %div.269), kind=kOutput, calls=%fused_computation.9 | convolution fusion | flops 1348075520 | bytes 13643776 | tf_op jit(solution)/shard_map/dot_general | solution.py:78
  131.6 2.1 copy.39
  133.9 1.5 slice.147
  136.1 2.9 %copy.55 = f32[256,2048]{1,0:T(8,128)} copy(f32[256,2048]{0,1:T(8,128)} %bitcast.286) | data formatting | bytes 4194304 | tf_op jit(solution)/shard_map/reshape | solution.py:67
  139.0 6.3 %convolution_add_fusion.6 = f32[256,2048]{1,0:T(8,128)} fusion(f32[256,2048]{1,0:T(8,128)} %copy.55, f32[512,2048]{1,0:T(8,128)} %bitcast.274, f32[512]{0:T(512)S(1)} %get-tuple-element.59, f32[2048]{0:T(1024)S(1)} %bitcast.296, f32[5,256,512]{1,2,0:T(8,128)S(1)} %bitcast.258, f32[512]{0:T(512)S(1)} %broadcast_multiply_fusion.14, ...), kind=kOutput, calls=%fused_computation.19 | convolution fusion | flops 1079377920 | bytes 11552768 | tf_op jit(solution)/shard_map/dot_general | solution.py:78
  145.3 2.9 %copy.56 = f32[256,2048]{0,1:T(8,128)} copy(f32[256,2048]{1,0:T(8,128)} %convolution_add_fusion.6) | data formatting | bytes 4194304 | tf_op jit(solution)/shard_map/reshape | solution.py:81
  148.2 2.8 %slice.152 = f32[3,256,512]{1,2,0:T(8,128)} slice(f32[4,256,512]{1,2,0:T(8,128)} %bitcast.260), slice={[1:4], [0:256], [0:512]} | slice | bytes 3145728 | tf_op jit(solution)/shard_map/slice | solution.py:67
  151.5 3.0 %copy.46 = f32[256,1536]{1,0:T(8,128)} copy(f32[256,1536]{0,1:T(8,128)} %bitcast.275) | data formatting | bytes 3145728 | tf_op jit(solution)/shard_map/reshape | solution.py:67
  154.5 1.3 multiply_reduce_fusion.3
  155.8 5.5 %convolution_add_fusion.1 = f32[256,1536]{1,0:T(8,128)} fusion(f32[256,1536]{1,0:T(8,128)} %copy.46, f32[512,1536]{1,0:T(8,128)} %copy.45, f32[512]{0:T(512)S(1)} %get-tuple-element.55, f32[256,1536]{0,1:T(8,128)} %bitcast.276, f32[1536]{0:T(1024)S(1)} %div.290, f32[4,256,512]{1,2,0:T(8,128)} %bitcast.262, f32[512]{0:T(512)S(1)} %broadcast_multiply_fusion.13, ...), kind=kOutput, calls=%fused_computation.14 | convolution fusion | flops 809762816 | bytes 8931328 | tf_op jit(solution)/shard_map/dot_general | solution.py:78
  161.4 3.1 %copy.47 = f32[256,1536]{0,1:T(8,128)} copy(f32[256,1536]{1,0:T(8,128)} %convolution_add_fusion.1) | data formatting | bytes 3145728 | tf_op jit(solution)/shard_map/add | solution.py:78
  164.4 2.4 %slice.157 = f32[2,256,512]{1,2,0:T(8,128)} slice(f32[3,256,512]{1,2,0:T(8,128)} %bitcast.266), slice={[1:3], [0:256], [0:512]} | slice | bytes 2097152 | tf_op jit(solution)/shard_map/slice | solution.py:67
  167.2 2.6 %copy.57 = f32[256,1024]{1,0:T(8,128)} copy(f32[256,1024]{0,1:T(8,128)} %bitcast.288) | data formatting | bytes 2097152 | tf_op jit(solution)/shard_map/reshape | solution.py:67
  169.8 1.3 multiply_reduce_fusion.2
  171.1 4.4 %fusion.5 = f32[256,1024]{1,0:T(8,128)} fusion(f32[256,1024]{1,0:T(8,128)} %copy.57, f32[512,1024]{1,0:T(8,128)} %bitcast.285, f32[512]{0:T(512)S(1)} %get-tuple-element.51, f32[1024]{0:T(1024)S(1)} %bitcast.297, f32[3,256,512]{1,2,0:T(8,128)} %bitcast.268, f32[512]{0:T(512)S(1)} %broadcast_multiply_fusion.12, f32[512]{0:T(512)S(1)} %get-tuple-element.53, ...), kind=kOutput, calls=%fused_computation.39 | convolution fusion | flops 540147712 | bytes 6305792 | tf_op jit(solution)/shard_map/dot_general | solution.py:78
  175.5 1.3 copy.74
  177.4 0.6 fusion.8
  178.0 1.1 fusion.123
  179.2 4.2 %fusion.111 = (f32[2048]{0:T(1024)S(1)}, f32[256,2048]{1,0:T(8,128)}) fusion(bf16[512,256]{1,0:T(8,128)(2,1)S(1)} %copy-done.7, bf16[512,256]{1,0:T(8,128)(2,1)S(1)} %get-tuple-element.9, f32[512]{0:T(512)S(1)} %get-tuple-element.64, bf16[256,2048]{1,0:T(8,128)(2,1)} %bitcast.284, f32[2048]{0:T(1024)S(1)} %broadcast_multiply_fusion.7), kind=kOutput, calls=%fused_computation.193 | convolution fusion | flops 1078982656 | bytes 3688448 | tf_op jit(solution)/shard_map/dot_general | solution.py:27
  183.4 4.9 %fusion.114 = (f32[2048]{0:T(1024)S(1)}, f32[256,2048]{1,0:T(8,128)}) fusion(f32[256,2048]{1,0:T(8,128)} %get-tuple-element.68, f32[512]{0:T(512)S(1)} %get-tuple-element.60, f32[2048]{0:T(1024)S(1)} %broadcast_multiply_fusion.6, f32[5,256,512]{1,2,0:T(8,128)S(1)} %bitcast.259, f32[512]{0:T(512)S(1)} %broadcast_multiply_fusion.14, ...), kind=kOutput, calls=%fused_computation.194 | convolution fusion | flops 1078851584 | bytes 7366656 | tf_op jit(solution)/shard_map/dot_general | solution.py:27
  188.3 5.4 %fusion.117 = (f32[2048]{0:T(1024)S(1)}, f32[256,2048]{1,0:T(8,128)}) fusion(f32[256,2048]{1,0:T(8,128)} %get-tuple-element.70, f32[512]{0:T(512)S(1)} %get-tuple-element.56, f32[2048]{0:T(1024)S(1)} %broadcast_multiply_fusion.5, f32[4,256,512]{1,2,0:T(8,128)} %bitcast.263, f32[512]{0:T(512)S(1)} %broadcast_multiply_fusion.13, ...), kind=kOutput, calls=%fused_computation.195 | convolution fusion | flops 1078851584 | bytes 7366656 | tf_op jit(solution)/shard_map/dot_general | solution.py:27
  193.7 5.0 %fusion.120 = (f32[2048]{0:T(1024)S(1)}, f32[256,2048]{1,0:T(8,128)}) fusion(f32[256,2048]{1,0:T(8,128)} %get-tuple-element.72, f32[512]{0:T(512)S(1)} %get-tuple-element.52, f32[2048]{0:T(1024)S(1)} %broadcast_multiply_fusion.4, f32[3,256,512]{1,2,0:T(8,128)S(1)} %bitcast.271, f32[512]{0:T(512)S(1)} %broadcast_multiply_fusion.12, ...), kind=kOutput, calls=%fused_computation.196 | convolution fusion | flops 1078851584 | bytes 7366656 | tf_op jit(solution)/shard_map/dot_general | solution.py:27
  198.7 5.0 %fusion.124 = (f32[2048]{0:T(1024)S(1)}, f32[256,2048]{1,0:T(8,128)}) fusion(f32[256,2048]{1,0:T(8,128)} %get-tuple-element.74, f32[512]{0:T(512)S(1)} %get-tuple-element.48, f32[2048]{0:T(1024)S(1)} %broadcast_multiply_fusion.3, f32[2,256,512]{2,1,0:T(8,128)S(1)} %bitcast.281, f32[512]{0:T(512)S(1)} %broadcast_multiply_fusion.11, ...), kind=kOutput, calls=%fused_computation.198 | convolution fusion | flops 1078851584 | bytes 7366656 | tf_op jit(solution)/shard_map/dot_general | solution.py:27
  203.8 3.6 %fusion.2 = bf16[256,2048]{1,0:T(8,128)(2,1)S(1)} fusion(f32[256,2048]{1,0:T(8,128)} %get-tuple-element.78, f32[512]{0:T(512)S(1)} %get-tuple-element.46, f32[2048]{0:T(1024)S(1)} %broadcast_multiply_fusion.2, f32[256,512]{1,0:T(8,128)S(1)} %copy-done.8, f32[512]{0:T(512)S(1)} %get-tuple-element.29, f32[512]{0:T(512)S(1)} %get-tuple-element.28, ...), kind=kOutput, calls=%fused_computation.25 | convolution fusion | flops 1078853632 | bytes 3686400 | tf_op jit(solution)/shard_map/dot_general | solution.py:27
  207.3 16.9 %all_to_all.38 = bf16[4,64,2048]{2,1,0:T(8,128)(2,1)S(1)} all-to-all(bf16[4,64,2048]{2,1,0:T(8,128)(2,1)S(1)} %bitcast.293), channel_id=1, replica_groups=mesh['groups'=2,'state'=4,'member'=4] {'member'}, dimensions={0} | all-to-all | bytes 2097152 | tf_op jit(solution)/shard_map/all_to_all | solution.py:83
  224.2 1.0 copy.65
  (112 shorter events, 7.6 us)
Async XLA Ops:
  6.5 6.6 %copy-start.10 = (s32[6,1,8]{2,1,0:T(1,128)S(1)}, s32[6,1,8]{2,1,0:T(1,128)}, u32[]{:S(2)}) copy-start(s32[6,1,8]{2,1,0:T(1,128)} %param.9) | copy-start | bytes 580
  6.5 6.6 %copy-start.11 = (f32[6,32]{1,0:T(8,128)S(1)}, f32[6,32]{1,0:T(8,128)}, u32[]{:S(2)}) copy-start(f32[6,32]{1,0:T(8,128)} %param.7) | copy-start | bytes 2308
  6.5 53.2 %copy-start.12 = (f32[6,32]{1,0:T(8,128)S(1)}, f32[6,32]{1,0:T(8,128)}, u32[]{:S(2)}) copy-start(f32[6,32]{1,0:T(8,128)} %param.6) | copy-start | bytes 2308
  6.5 72.1 %copy-start.9 = (s32[6,32]{1,0:T(8,128)S(1)}, s32[6,32]{1,0:T(8,128)}, u32[]{:S(2)}) copy-start(s32[6,32]{1,0:T(8,128)} %param.8) | copy-start | bytes 2308
  8.9 70.4 %all-to-all-start = ((bf16[64,4,2048]{2,0,1:T(8,128)(2,1)}), bf16[64,4,2048]{2,0,1:T(8,128)(2,1)S(1)}, u32[]{:S(2)}, u32[]{:S(2)}) async-start(bf16[64,4,2048]{2,0,1:T(8,128)(2,1)} %bitcast.251), calls=%async_computation | async-start | bytes 2097152 | tf_op jit(solution)/shard_map/all_to_all | solution.py:33
  13.1 105.6 %all-gather.4.cloned.1.call-start = ((), (), s32[]{:S(2)}) async-start(), calls=%async_computation.2 | async-start | bytes 1671168 | tf_op jit(solution)/shard_map/all_gather | solution.py:43
  79.3 3.3 %copy-start.5 = (bf16[64,4,2048]{2,0,1:T(8,128)(2,1)}, bf16[64,4,2048]{2,0,1:T(8,128)(2,1)S(1)}, u32[]{:S(2)}) copy-start(bf16[64,4,2048]{2,0,1:T(8,128)(2,1)S(1)} %all-to-all-done) | copy-start | bytes 3145732
  103.1 2.5 %copy-start.6 = (bf16[64,4,2048]{2,0,1:T(8,128)(2,1)S(1)}, bf16[64,4,2048]{2,0,1:T(8,128)(2,1)}, u32[]{:S(2)}) copy-start(bf16[64,4,2048]{2,0,1:T(8,128)(2,1)} %copy-done.5) | copy-start | bytes 3145732
  148.2 2.8 %copy-start = (f32[256,2048]{0,1:T(8,128)S(1)}, f32[256,2048]{0,1:T(8,128)}, u32[]{:S(2)}) copy-start(f32[256,2048]{0,1:T(8,128)} %copy.56) | copy-start | bytes 6291460
  164.4 2.4 %copy-start.1 = (f32[256,1536]{0,1:T(8,128)S(1)}, f32[256,1536]{0,1:T(8,128)}, u32[]{:S(2)}) copy-start(f32[256,1536]{0,1:T(8,128)} %copy.47) | copy-start | bytes 4718596
  176.8 1.2 copy-start.3
  177.4 1.8 copy-start.7
  188.3 5.4 %copy-start.2 = (f32[256,1536]{0,1:T(8,128)S(1)}, f32[256,1536]{0,1:T(8,128)}, u32[]{:S(2)}) copy-start(f32[256,1536]{0,1:T(8,128)} %copy.47) | copy-start | bytes 4718596
  193.7 5.0 %copy-start.4 = (f32[32,2,8,512]{3,2,0,1:T(8,128)S(1)}, f32[32,2,8,512]{3,2,0,1:T(8,128)}, u32[]{:S(2)}) copy-start(f32[32,2,8,512]{3,2,0,1:T(8,128)} %copy-done.3) | copy-start | bytes 3145732
  198.7 5.0 %copy-start.8 = (f32[256,512]{1,0:T(8,128)S(1)}, f32[256,512]{1,0:T(8,128)}, u32[]{:S(2)}) copy-start(f32[256,512]{1,0:T(8,128)} %get-tuple-element.76) | copy-start | bytes 1572868
Sparse Core Ops, SparseCore 0:
  81.7 36.9 all-gather.3
where the time goes:
time: 233 us; the launch traced here: 232 us
  blocking collectives  82.4 us (35%)
  matrix products  57.1 us (25%)
  local copies, waits for them, and re-layouts  52.7 us (23%)
  between operations  13.8 us (6%)
  waiting for transfers between devices  13 us (6%)
  other arithmetic  8.98 us (4%)
  starting transfers between devices  4.21 us (2%)
    all_gather x1, blocking collectives, per_device(): lax.all_gather(obs_var, ('state', 'member'), axis=1, tiled=True)  29 us
    dot_general x6, matrix products, apply_rows(): lax.dot_general(incr, weights, (((0,), (0,)), ((), ())), preferred_elemen...  28 us
    dot_general x5, matrix products, per_device(): lax.dot_general(incr, weights, (((0,), (0,)), ((), ())), preferred_elemen...  24.2 us
    all_gather x1, blocking collectives, per_device(): lax.all_gather(obs_value, ('state', 'member'), axis=1, tiled=True)  18.9 us
    all_gather x1, blocking collectives, per_device(): lax.all_gather(loc_pattern.astype(jnp.bfloat16), ('state', 'member'), axi...  17.5 us
    all_to_all x1, blocking collectives, per_device(): lax.all_to_all(state.astype(jnp.bfloat16), 'member', split_axis=0, concat...  16.9 us
    another operation x6, local copies, waits for them, and re-layouts, per_device(): wmat = jnp.tile(col_loc.T, (1, BATCHES - batch - 1))  13.1 us
    all_gather x1, waiting for transfers between devices, per_device(): lax.all_gather(own_cols, ('state', 'member'), axis=1, tiled=True)  13 us
  transfers between devices with their start and end apart: 2, of which 1 were waited for; matrix products, arithmetic and copies ran while one was open for 11% of the time, Pallas kernels for 0%

commit v1 on v0

--- a/solution.py
+++ b/solution.py
@@ -1,6 +1,10 @@
+import functools
+
 import jax
 import jax.numpy as jnp
 from jax import lax
+from jax.experimental import pallas as pl
+from jax.experimental.pallas import tpu as pltpu
 from jax.sharding import PartitionSpec as P
 
 BATCHES = 6
@@ -85,6 +89,276 @@
     )
 
 
+LANES = 128
+MESH = pl.DeviceIdType.MESH
+
+
+def row_mean(values):
+    return jnp.mean(values, axis=1, keepdims=True)
+
+
+def ensemble_kernel(
+    nz, own, ens_ref, meta_ref, out_ref,
+    meta, cols, every, state, qstate, vals, lxs, qsend, qrecv,
+    meta_s, meta_r, z_s, z_r, x_s, x_r, c_s, c_r, d_s, d_r,
+    ex_s, ex_r, ec_s, ec_r, ed_s, ed_r, q_s, q_r, local_s,
+):
+    f32, bf16 = jnp.float32, jnp.bfloat16
+    nm = 4
+    rows, width = ens_ref.shape
+    block = width // nm
+    members = rows * nm
+    nobs = nz * nm * own
+    z, m = lax.axis_index("state"), lax.axis_index("member")
+
+    def peer(dz, dm):
+        return {"state": lax.rem(z + dz, nz), "member": jnp.bitwise_xor(m, dm)}
+
+    def send(src, dst, ssem, rsem, dz, dm):
+        copy = pltpu.make_async_remote_copy(
+            src_ref=src, dst_ref=dst, send_sem=ssem, recv_sem=rsem,
+            device_id=peer(dz, dm), device_id_type=MESH,
+        )
+        copy.start()
+        sent.append(copy)
+        return copy
+
+    sent = []
+    others = [(dz, dm) for dz in range(nz) for dm in range(nm) if dz or dm]
+    barrier = pltpu.get_barrier_semaphore()
+    for dz, dm in others:
+        pl.semaphore_signal(barrier, inc=1, device_id=peer(dz, dm), device_id_type=MESH)
+    pl.semaphore_wait(barrier, len(others))
+
+    mine = z * nm + m
+    meta[mine] = meta_ref[...]
+    meta_copies = {}
+    for dz, dm in others:
+        at = dz * nm + dm
+        meta_copies[dz, dm] = send(meta.at[mine], meta.at[mine], meta_s.at[at], meta_r.at[at], dz, dm)
+    base = pl.multiple_of(m * rows, rows)
+    base_x = pl.multiple_of(jnp.bitwise_xor(m, 2) * rows, rows)
+    keep = pltpu.make_async_copy(ens_ref, every.at[pl.ds(base, rows), :], local_s)
+    keep.start()
+    for dm in range(1, nm):
+        meta_copies[0, dm].wait_recv()
+
+    site_iota = lax.broadcasted_iota(jnp.int32, (block, LANES), 0).astype(f32)
+    first, second = [], []
+    for kk in range(nm):
+        got = meta[z * nm + kk]
+        piece = ens_ref[:, kk * block : (kk + 1) * block]
+        for out, r in ((first, 6), (second, 7)):
+            onehot = jnp.where(site_iota == got[r : r + 1, :], 1.0, 0.0).astype(bf16)
+            out.append(jnp.dot(piece, onehot, preferred_element_type=f32).astype(bf16))
+    r_iota = lax.broadcasted_iota(jnp.int32, (nm * LANES, nm * LANES), 0)
+    c_iota = lax.broadcasted_iota(jnp.int32, (nm * LANES, nm * LANES), 1)
+    target = (r_iota % LANES) // own * LANES + r_iota // LANES * own + r_iota % own
+    perm = jnp.where(c_iota == target, 1.0, 0.0).astype(bf16)
+    placed = jnp.dot(jnp.concatenate(first, axis=1), perm, preferred_element_type=f32).astype(bf16)
+    placed2 = jnp.dot(
+        jnp.concatenate(second, axis=1), perm[:, : 2 * LANES], preferred_element_type=f32
+    ).astype(bf16)
+    cols[z, pl.ds(base, rows), 0 : nm * LANES] = placed
+    cols[z, pl.ds(base, rows), nm * LANES : BATCHES * LANES] = placed2
+
+    chunks = (pl.ds(0, LANES), pl.ds(LANES, (BATCHES - 1) * LANES))
+
+    def view(d, c, start):
+        return cols.at[lax.rem(z - d + nz, nz), pl.ds(start, rows), chunks[c]]
+
+    zc, xc, cc, dc = {}, {}, {}, {}
+
+    def forward(c, d):
+        at = c * nz + d
+        v = view(d, c, base)
+        xc[c, d] = send(v, v, x_s.at[at], x_r.at[at], 0, 2)
+        cc[c, d] = send(v, v, c_s.at[at], c_r.at[at], 0, 1)
+
+    def relay(c, d):
+        at = c * nz + d
+        xc[c, d].wait_recv()
+        v = view(d, c, base_x)
+        dc[c, d] = send(v, v, d_s.at[at], d_r.at[at], 0, 1)
+
+    for c in range(2):
+        v = view(0, c, base)
+        for d in range(1, nz):
+            at = c * nz + d
+            zc[c, d] = send(v, v, z_s.at[at], z_r.at[at], d, 0)
+        forward(c, 0)
+
+    for dz, dm in others:
+        if dz:
+            meta_copies[dz, dm].wait_recv()
+    for k in range(nz * nm):
+        turned = meta[k].T
+        vals[0, k * own : (k + 1) * own, :] = turned[0:own, :]
+        vals[1, k * own : (k + 1) * own, :] = turned[own : 2 * own, :]
+    ntiles = 8
+    er = lax.broadcasted_iota(jnp.int32, (LANES, nobs), 0)
+    ec = lax.broadcasted_iota(jnp.int32, (LANES, nobs), 1)
+    expand = jnp.where(er == ec // (nobs // ntiles) + 2 * own, 1.0, 0.0).astype(bf16)
+    own_loc = jnp.dot(meta_ref[...].astype(bf16), expand, preferred_element_type=f32)
+    wide = jnp.dot(
+        meta[...].reshape(nz * nm * 8, LANES).astype(bf16), expand, preferred_element_type=f32
+    ).reshape(nz * nm, 8, nobs)
+    for b in range(BATCHES):
+        lxs[b] = wide[:, b, :]
+
+    for d in range(1, nz):
+        zc[0, d].wait_recv()
+        forward(0, d)
+    for d in range(nz):
+        relay(0, d)
+    for d in range(1, nz):
+        zc[1, d].wait_recv()
+        forward(1, d)
+
+    exc, ecc, edc = {}, {}, {}
+    for kk in range(nm):
+        part = pl.ds(kk * block, block)
+        there = every.at[pl.ds(base, rows), part]
+        exc[kk] = send(ens_ref.at[:, part], there, ex_s.at[kk], ex_r.at[kk], 0, 2)
+        ecc[kk] = send(ens_ref.at[:, part], there, ec_s.at[kk], ec_r.at[kk], 0, 1)
+
+    def relay_ens(kk):
+        exc[kk].wait_recv()
+        there = every.at[pl.ds(base_x, rows), pl.ds(kk * block, block)]
+        edc[kk] = send(there, there, ed_s.at[kk], ed_r.at[kk], 0, 1)
+
+    def arrive(c):
+        for d in range(nz):
+            cc[c, d].wait_recv()
+            dc[c, d].wait_recv()
+
+    def unpack(b):
+        for zz in range(nz):
+            got = cols[zz, :, b * LANES : (b + 1) * LANES].astype(f32)
+            state[b, zz * LANES : (zz + 1) * LANES, :] = got.T
+
+    qr = lax.broadcasted_iota(jnp.int32, (members, members), 0)
+    qc = lax.broadcasted_iota(jnp.int32, (members, members), 1)
+    eye = jnp.where(qr == qc, 1.0, 0.0)
+    contract = (((1,), (1,)), ((), ()))
+
+    arrive(0)
+    unpack(0)
+    for b in range(BATCHES):
+        prior = state[b]
+        ovar, oval = vals[1, :, b : b + 1], vals[0, :, b : b + 1]
+        ymean = row_mean(prior)
+        yanom = prior - ymean
+        spread = jnp.sum(yanom * yanom, axis=1, keepdims=True) / (members - 1.0)
+        post_mean = (ymean * ovar + oval * spread) / (ovar + spread)
+        shrink = jnp.sqrt(ovar / (ovar + spread))
+        incr = (post_mean + shrink * yanom - prior).astype(bf16)
+        gain = 1.0 / ((members - 1.0) * (spread + EPS))
+        ygain = (yanom * gain).astype(bf16)
+
+        if b == 0:
+            weights = (lax.dot_general(eye.astype(bf16), ygain, contract, preferred_element_type=f32)
+                       * own_loc[0:1, :]).astype(bf16)
+            qstate[...] = jnp.dot(weights, incr, preferred_element_type=f32)
+            for d in range(nz):
+                relay(1, d)
+            arrive(1)
+            for later in range(1, BATCHES):
+                unpack(later)
+        else:
+            q = qstate[...]
+            xanom = (q - row_mean(q) + eye).astype(bf16)
+            weights = (lax.dot_general(xanom, ygain, contract, preferred_element_type=f32)
+                       * own_loc[b : b + 1, :]).astype(bf16)
+            qstate[...] = q + jnp.dot(weights, incr, preferred_element_type=f32)
+
+        if b + 1 < BATCHES:
+            local = lxs[b]
+
+            @pl.loop(b + 1, BATCHES)
+            def _(later):
+                x = state[later]
+                xanom = (x - row_mean(x)).astype(bf16)
+                cov = lax.dot_general(xanom, ygain, contract, preferred_element_type=f32)
+                cov = cov.reshape(nz * nm, own, nobs) * local[:, None, :]
+                weights = cov.reshape(nobs, nobs).astype(bf16)
+                state[later] = x + jnp.dot(weights, incr, preferred_element_type=f32)
+
+        if 1 <= b <= nm - 1:
+            relay_ens(b - 1)
+
+    q = qstate[...]
+    q = (q - jnp.mean(q, axis=0, keepdims=True)).T.astype(bf16)
+    qsend[...] = q
+    qrecv[m] = qsend[pl.ds(base, rows), :]
+    qcs = []
+    for dm in range(1, nm):
+        to = pl.multiple_of(jnp.bitwise_xor(m, dm) * rows, rows)
+        qcs.append(send(qsend.at[pl.ds(to, rows), :], qrecv.at[m], q_s.at[dm], q_r.at[dm], 0, dm))
+    relay_ens(nm - 1)
+    keep.wait()
+    for copy in qcs:
+        copy.wait_recv()
+    for kk in range(nm):
+        ecc[kk].wait_recv()
+        edc[kk].wait_recv()
+        part = slice(kk * block, (kk + 1) * block)
+        delta = jnp.dot(qrecv[kk], every[:, part], preferred_element_type=f32)
+        out_ref[:, part] = (ens_ref[:, part].astype(f32) + delta).astype(bf16)
+    for copy in sent:
+        copy.wait_send()
+
+
+def per_device_kernel(nz, ensemble, obs_value, obs_var, obs_site, loc_pattern):
+    nm = 4
+    own = obs_site.shape[1]
+    rows, width = ensemble.shape
+    members, nobs, block = rows * nm, nz * nm * own, width // nm
+    loc = loc_pattern[:, 0, :].astype(jnp.float32)
+    head = jnp.concatenate([obs_value, obs_var, loc], axis=1)
+    head = jnp.pad(head, ((0, 0), (0, LANES - head.shape[1])))
+    sites = obs_site.astype(jnp.float32).reshape(-1)
+    sites = jnp.pad(sites, (0, 2 * LANES - sites.shape[0]), constant_values=-1.0)
+    meta = jnp.concatenate([head, sites.reshape(2, LANES)], axis=0)
+    dma, bf16, f32 = pltpu.SemaphoreType.DMA, jnp.bfloat16, jnp.float32
+    two = [dma((2 * nz,))] * 2
+    return pl.pallas_call(
+        functools.partial(ensemble_kernel, nz, own),
+        out_shape=jax.ShapeDtypeStruct(ensemble.shape, bf16),
+        in_specs=[pl.BlockSpec(memory_space=pltpu.VMEM)] * 2,
+        out_specs=pl.BlockSpec(memory_space=pltpu.VMEM),
+        scratch_shapes=[
+            pltpu.VMEM((nz * nm, 8, LANES), f32),
+            pltpu.VMEM((nz, members, BATCHES * LANES), bf16),
+            pltpu.VMEM((members, width), bf16),
+            pltpu.VMEM((BATCHES, nobs, members), f32),
+            pltpu.VMEM((members, members), f32),
+            pltpu.VMEM((2, nobs, 8), f32),
+            pltpu.VMEM((BATCHES, nz * nm, nobs), f32),
+            pltpu.VMEM((members, members), bf16),
+            pltpu.VMEM((nm, rows, members), bf16),
+            dma((nz * nm,)), dma((nz * nm,)),
+            *two, *two, *two, *two,
+            *[dma((nm,))] * 8,
+            dma,
+        ],
+        compiler_params=pltpu.CompilerParams(
+            collective_id=0, has_side_effects=True, vmem_limit_bytes=48 * 2**20
+        ),
+    )(ensemble, meta)
+
+
+def dispatch(nz, nm, ensemble, obs_value, obs_var, obs_site, loc_pattern):
+    own = obs_site.shape[1]
+    fits = (
+        nm == 4 and own * nm == LANES and obs_site.shape[0] == BATCHES and loc_pattern.shape[1:] == (1, 8)
+        and ensemble.shape[0] % 16 == 0 and ensemble.shape[1] % (nm * LANES) == 0
+    )
+    if fits:
+        return per_device_kernel(nz, ensemble, obs_value, obs_var, obs_site, loc_pattern)
+    return per_device(ensemble, obs_value, obs_var, obs_site, loc_pattern)
+
+
 def solution(mesh):
     in_specs = (
         P("member", ("groups", "state")),
@@ -94,6 +368,7 @@
         P(None, ("groups", "state", "member"), None),
     )
     out_specs = P("member", ("groups", "state"))
+    sizes = (mesh.shape["state"], mesh.shape["member"])
     return jax.shard_map(
-        per_device, mesh=mesh, in_specs=in_specs, out_specs=out_specs, check_vma=False
-    )
+        functools.partial(dispatch, *sizes), mesh=mesh, in_specs=in_specs, out_specs=out_specs, check_vma=False
+    )

time: 233 us -> 55.1 us (0.24)
  blocking collectives: 82.4 us -> 0 us
  matrix products: 57.1 us -> 0 us
  Pallas kernels: 0 us -> 50.5 us
  local copies, waits for them, and re-layouts: 52.7 us -> 3.56 us
  between operations: 13.8 us -> 0.02 us
  waiting for transfers between devices: 13 us -> 0 us
  other arithmetic: 8.98 us -> 0.78 us
  starting transfers between devices: 4.21 us -> 0 us
    all_gather x3 -> x0, blocking collectives: 65.5 us -> none  [the longest x1 29 us: per_device(): lax.all_gather(obs_var, ('state', 'member'), axis=1, tiled=True)]
    dot_general x22 -> x0, matrix products: 57.1 us -> none  [the longest x6 28 us: apply_rows(): lax.dot_general(incr, weights, (((0,), (0,)), ((), ())), preferred_elemen...]
    pallas_call x0 -> x1, Pallas kernels: none -> 50.5 us  [per_device_kernel(): pl.pallas_call(functools.partial(ensemble_kernel, nz, own), out_shape=jax...]
    all_to_all x1 -> x0, blocking collectives: 16.9 us -> none  [per_device(): lax.all_to_all(state.astype(jnp.bfloat16), 'member', split_axis=0, concat...]
    reshape x14 -> x2, local copies, waits for them, and re-layouts: 15.4 us -> 0.08 us  [the longest x1 0.08 us: per_device_kernel(): sites = obs_site.astype(jnp.float32).reshape(-1)]
    another operation x6 -> x0, local copies, waits for them, and re-layouts: 13.1 us -> none  [per_device(): wmat = jnp.tile(col_loc.T, (1, BATCHES - batch - 1))]
    all_gather x1 -> x0, waiting for transfers between devices: 13 us -> none  [per_device(): lax.all_gather(own_cols, ('state', 'member'), axis=1, tiled=True)]
    slice x7 -> x0, local copies, waits for them, and re-layouts: 7.12 us -> none  [the longest x4 7.06 us: per_device(): later = columns[batch + 1:].transpose(1, 0, 2).reshape(members, -1)]
  transfers between devices with their start and end apart: 2 -> 0, of which waited for: 1 -> 0; matrix products, arithmetic and copies ran while one was open for 11% -> 0% of each run, Pallas kernels for 0% -> 0%
where the time goes in v1:
time: 55.1 us; the launch traced here: 54.8 us
  Pallas kernels  50.5 us (92%)
  local copies, waits for them, and re-layouts  3.56 us (6%)
  other arithmetic  0.78 us (1%)
    pallas_call x1, Pallas kernels, per_device_kernel(): pl.pallas_call(functools.partial(ensemble_kernel, nz, own), out_shape=jax...  50.5 us
    unnamed x9, local copies, waits for them, and re-layouts  3.47 us

profile of v1, /device:TPU:0, one launch (start us, length us, event | category | flops | bytes accessed | tf_op | source)
XLA Modules:
  0.0 54.8 jit_solution(1340062270385725812)
XLA Ops:
  0.0 0.7 %convert_element_type.13 = f32[6,32]{1,0:T(8,128)S(1)} convert(s32[6,32]{1,0:T(8,128)} %param.8) | non-fusion elementwise | flops 192 | bytes 1536 | tf_op jit(solution)/shard_map/convert_element_type | solution.py:320
  0.7 0.0 copy-start.3
  0.7 0.1 reshape.7
  0.8 0.0 copy-start.2
  0.8 0.6 %copy-done.3 = s32[6,1,8]{2,1,0:T(1,128)S(1)} copy-done((s32[6,1,8]{2,1,0:T(1,128)S(1)}, s32[6,1,8]{2,1,0:T(1,128)}, u32[]{:S(2)}) %copy-start.3) | copy-done | bytes 216
  1.4 0.0 copy-start.1
  1.4 0.1 copy-done.2
  1.5 0.6 %copy-done.1 = f32[6,32]{1,0:T(8,128)S(1)} copy-done((f32[6,32]{1,0:T(8,128)S(1)}, f32[6,32]{1,0:T(8,128)}, u32[]{:S(2)}) %copy-start.1) | copy-done | bytes 792
  2.1 0.1 select_maximum_fusion
  2.1 0.0 copy-start
  2.2 1.2 %copy-done = bf16[64,8192]{1,0:T(8,128)(2,1)S(1)} copy-done((bf16[64,8192]{1,0:T(8,128)(2,1)S(1)}, bf16[64,8192]{1,0:T(8,128)(2,1)}, u32[]{:S(2)}) %copy-start) | copy-done | bytes 1048600
  3.4 50.5 %shard_map.55 = bf16[64,8192]{1,0:T(8,128)(2,1)S(1)} custom-call(bf16[64,8192]{1,0:T(8,128)(2,1)S(1)} %copy-done, f32[8,128]{1,0:T(8,128)S(1)} %pad_maximum_fusion.meta_ref), custom_call_target="tpu_custom_call" | custom-call | tf_op jit(solution)/shard_map/pallas_call | solution.py:325
  53.9 1.0 %copy.11 = bf16[64,8192]{1,0:T(8,128)(2,1)} copy(bf16[64,8192]{1,0:T(8,128)(2,1)S(1)} %shard_map.55) | data formatting | bytes 2097152
  (3 shorter events, 0.0 us)
Async XLA Ops:
  0.7 0.7 %copy-start.3 = (s32[6,1,8]{2,1,0:T(1,128)S(1)}, s32[6,1,8]{2,1,0:T(1,128)}, u32[]{:S(2)}) copy-start(s32[6,1,8]{2,1,0:T(1,128)} %param.9) | copy-start | bytes 580
  0.8 0.7 %copy-start.2 = (f32[6,32]{1,0:T(8,128)S(1)}, f32[6,32]{1,0:T(8,128)}, u32[]{:S(2)}) copy-start(f32[6,32]{1,0:T(8,128)} %param.6) | copy-start | bytes 2308
  1.4 0.7 %copy-start.1 = (f32[6,32]{1,0:T(8,128)S(1)}, f32[6,32]{1,0:T(8,128)}, u32[]{:S(2)}) copy-start(f32[6,32]{1,0:T(8,128)} %param.7) | copy-start | bytes 2308
  2.1 1.2 %copy-start = (bf16[64,8192]{1,0:T(8,128)(2,1)S(1)}, bf16[64,8192]{1,0:T(8,128)(2,1)}, u32[]{:S(2)}) copy-start(bf16[64,8192]{1,0:T(8,128)(2,1)} %ens_ref.1) | copy-start | bytes 3145732

commit v2 on v1

--- a/solution.py
+++ b/solution.py
@@ -98,9 +98,10 @@
 
 
 def ensemble_kernel(
-    nz, own, ens_ref, meta_ref, out_ref,
-    meta, cols, every, state, qstate, vals, lxs, qsend, qrecv,
-    meta_s, meta_r, z_s, z_r, x_s, x_r, c_s, c_r, d_s, d_r,
+    nz, own, ens_ref, val_ref, var_ref, site_ref, loc_ref, out_ref,
+    meta, cols, every, state, ygains, incrs, qstate, vals, lxs, qsend, qrecv,
+    val_in, var_in, site_in, loc_in,
+    meta_s, meta_r, z_s, z_r, x_s, x_r, c_s, c_r,
     ex_s, ex_r, ec_s, ec_r, ed_s, ed_r, q_s, q_r, local_s,
 ):
     f32, bf16 = jnp.float32, jnp.bfloat16
@@ -123,23 +124,60 @@
         sent.append(copy)
         return copy
 
+    def place(member):
+        return pl.multiple_of((member % 2 * 2 + member // 2) * rows, rows)
+
+    base = place(m)
+    pair = pl.multiple_of(m % 2 * (2 * rows), 2 * rows)
+    pair_c = pl.multiple_of((1 - m % 2) * (2 * rows), 2 * rows)
+    base_x = place(jnp.bitwise_xor(m, 2))
+    loads = [
+        pltpu.make_async_copy(src, dst, local_s.at[at])
+        for at, (src, dst) in enumerate((
+            (val_ref, val_in), (var_ref, var_in), (site_ref, site_in), (loc_ref, loc_in),
+            (ens_ref, every.at[pl.ds(base, rows), :]),
+        ))
+    ]
+    for copy in loads:
+        copy.start()
+
     sent = []
     others = [(dz, dm) for dz in range(nz) for dm in range(nm) if dz or dm]
     barrier = pltpu.get_barrier_semaphore()
     for dz, dm in others:
         pl.semaphore_signal(barrier, inc=1, device_id=peer(dz, dm), device_id_type=MESH)
+    for copy in loads[:4]:
+        copy.wait()
+    mine = z * nm + m
+    loc = loc_in[:, 0, :].astype(f32)
+    sites = [site_in[b : b + 1, :].astype(f32) for b in range(BATCHES)]
+    spare = LANES - 2 * own - loc.shape[1]
+    meta[mine, 0:BATCHES, :] = jnp.concatenate(
+        [val_in[...], var_in[...], loc, jnp.zeros((BATCHES, spare), f32)], axis=1
+    )
+    meta[mine, 6:7, :] = jnp.concatenate(sites[:4], axis=1)
+    meta[mine, 7:8, :] = jnp.concatenate(
+        sites[4:] + [jnp.full((1, LANES - 2 * own), -1.0, f32)], axis=1
+    )
     pl.semaphore_wait(barrier, len(others))
-
-    mine = z * nm + m
-    meta[mine] = meta_ref[...]
     meta_copies = {}
     for dz, dm in others:
         at = dz * nm + dm
         meta_copies[dz, dm] = send(meta.at[mine], meta.at[mine], meta_s.at[at], meta_r.at[at], dz, dm)
-    base = pl.multiple_of(m * rows, rows)
-    base_x = pl.multiple_of(jnp.bitwise_xor(m, 2) * rows, rows)
-    keep = pltpu.make_async_copy(ens_ref, every.at[pl.ds(base, rows), :], local_s)
-    keep.start()
+    loads[4].wait()
+    exc, ecc, edc = {}, {}, {}
+
+    def send_ens(kk):
+        there = every.at[pl.ds(base, rows), pl.ds(kk * block, block)]
+        exc[kk] = send(there, there, ex_s.at[kk], ex_r.at[kk], 0, 2)
+        ecc[kk] = send(there, there, ec_s.at[kk], ec_r.at[kk], 0, 1)
+
+    def relay_ens(kk):
+        exc[kk].wait_recv()
+        there = every.at[pl.ds(base_x, rows), pl.ds(kk * block, block)]
+        edc[kk] = send(there, there, ed_s.at[kk], ed_r.at[kk], 0, 1)
+
+    send_ens(0)
     for dm in range(1, nm):
         meta_copies[0, dm].wait_recv()
 
@@ -147,7 +185,7 @@
     first, second = [], []
     for kk in range(nm):
         got = meta[z * nm + kk]
-        piece = ens_ref[:, kk * block : (kk + 1) * block]
+        piece = every[pl.ds(base, rows), kk * block : (kk + 1) * block]
         for out, r in ((first, 6), (second, 7)):
             onehot = jnp.where(site_iota == got[r : r + 1, :], 1.0, 0.0).astype(bf16)
             out.append(jnp.dot(piece, onehot, preferred_element_type=f32).astype(bf16))
@@ -162,31 +200,43 @@
     cols[z, pl.ds(base, rows), 0 : nm * LANES] = placed
     cols[z, pl.ds(base, rows), nm * LANES : BATCHES * LANES] = placed2
 
-    chunks = (pl.ds(0, LANES), pl.ds(LANES, (BATCHES - 1) * LANES))
-
-    def view(d, c, start):
-        return cols.at[lax.rem(z - d + nz, nz), pl.ds(start, rows), chunks[c]]
-
-    zc, xc, cc, dc = {}, {}, {}, {}
-
-    def forward(c, d):
-        at = c * nz + d
-        v = view(d, c, base)
-        xc[c, d] = send(v, v, x_s.at[at], x_r.at[at], 0, 2)
-        cc[c, d] = send(v, v, c_s.at[at], c_r.at[at], 0, 1)
-
-    def relay(c, d):
-        at = c * nz + d
-        xc[c, d].wait_recv()
-        v = view(d, c, base_x)
-        dc[c, d] = send(v, v, d_s.at[at], d_r.at[at], 0, 1)
-
-    for c in range(2):
-        v = view(0, c, base)
+    chunks = ((0, 1), (1, 3), (3, BATCHES))
+
+    def view(d, c, start, count):
+        low, high = chunks[c]
+        lanes = pl.ds(low * LANES, (high - low) * LANES)
+        return cols.at[lax.rem(z - d + nz, nz), pl.ds(start, count), lanes]
+
+    zc, xc, cc = {}, {}, {}
+
+    def go_z(c, start, count):
+        v = view(0, c, start, count)
         for d in range(1, nz):
             at = c * nz + d
             zc[c, d] = send(v, v, z_s.at[at], z_r.at[at], d, 0)
-        forward(c, 0)
+
+    def go_x(c, d):
+        at, v = c * nz + d, view(d, c, base, rows)
+        xc[c, d] = send(v, v, x_s.at[at], x_r.at[at], 0, 2)
+
+    def go_core(c, d):
+        at, v = c * nz + d, view(d, c, pair, 2 * rows)
+        cc[c, d] = send(v, v, c_s.at[at], c_r.at[at], 0, 1)
+
+    def arrive(c):
+        for d in range(nz):
+            cc[c, d].wait_recv()
+
+    go_x(0, 0)
+    go_x(2, 0)
+    go_x(1, 0)
+    xc[0, 0].wait_recv()
+    go_z(0, pair, 2 * rows)
+    go_core(0, 0)
+    go_z(1, base, rows)
+    xc[2, 0].wait_recv()
+    go_z(2, pair, 2 * rows)
+    go_core(2, 0)
 
     for dz, dm in others:
         if dz:
@@ -199,7 +249,7 @@
     er = lax.broadcasted_iota(jnp.int32, (LANES, nobs), 0)
     ec = lax.broadcasted_iota(jnp.int32, (LANES, nobs), 1)
     expand = jnp.where(er == ec // (nobs // ntiles) + 2 * own, 1.0, 0.0).astype(bf16)
-    own_loc = jnp.dot(meta_ref[...].astype(bf16), expand, preferred_element_type=f32)
+    own_loc = jnp.dot(meta[mine].astype(bf16), expand, preferred_element_type=f32)
     wide = jnp.dot(
         meta[...].reshape(nz * nm * 8, LANES).astype(bf16), expand, preferred_element_type=f32
     ).reshape(nz * nm, 8, nobs)
@@ -208,29 +258,12 @@
 
     for d in range(1, nz):
         zc[0, d].wait_recv()
-        forward(0, d)
-    for d in range(nz):
-        relay(0, d)
+        go_core(0, d)
     for d in range(1, nz):
         zc[1, d].wait_recv()
-        forward(1, d)
-
-    exc, ecc, edc = {}, {}, {}
-    for kk in range(nm):
-        part = pl.ds(kk * block, block)
-        there = every.at[pl.ds(base, rows), part]
-        exc[kk] = send(ens_ref.at[:, part], there, ex_s.at[kk], ex_r.at[kk], 0, 2)
-        ecc[kk] = send(ens_ref.at[:, part], there, ec_s.at[kk], ec_r.at[kk], 0, 1)
-
-    def relay_ens(kk):
-        exc[kk].wait_recv()
-        there = every.at[pl.ds(base_x, rows), pl.ds(kk * block, block)]
-        edc[kk] = send(there, there, ed_s.at[kk], ed_r.at[kk], 0, 1)
-
-    def arrive(c):
-        for d in range(nz):
-            cc[c, d].wait_recv()
-            dc[c, d].wait_recv()
+        go_x(1, d)
+    for kk in range(1, nm):
+        send_ens(kk)
 
     def unpack(b):
         for zz in range(nz):
@@ -242,9 +275,32 @@
     eye = jnp.where(qr == qc, 1.0, 0.0)
     contract = (((1,), (1,)), ((), ()))
 
-    arrive(0)
-    unpack(0)
     for b in range(BATCHES):
+        for c, (low, high) in enumerate(chunks):
+            if b == low:
+                if c == 1:
+                    for d in range(nz):
+                        xc[1, d].wait_recv()
+                        go_core(1, d)
+                if c == 2:
+                    for d in range(1, nz):
+                        zc[2, d].wait_recv()
+                        go_core(2, d)
+                    relay_ens(0)
+                arrive(c)
+                for fresh in range(low, high):
+                    unpack(fresh)
+
+        if b:
+            @pl.loop(0, b)
+            def _(earlier):
+                x = state[b]
+                xanom = (x - row_mean(x)).astype(bf16)
+                cov = lax.dot_general(xanom, ygains[earlier], contract, preferred_element_type=f32)
+                cov = cov.reshape(nz * nm, own, nobs) * lxs[earlier][:, None, :]
+                weights = cov.reshape(nobs, nobs).astype(bf16)
+                state[b] = x + jnp.dot(weights, incrs[earlier], preferred_element_type=f32)
+
         prior = state[b]
         ovar, oval = vals[1, :, b : b + 1], vals[0, :, b : b + 1]
         ymean = row_mean(prior)
@@ -255,37 +311,22 @@
         incr = (post_mean + shrink * yanom - prior).astype(bf16)
         gain = 1.0 / ((members - 1.0) * (spread + EPS))
         ygain = (yanom * gain).astype(bf16)
+        if b + 1 < BATCHES:
+            ygains[b] = ygain
+            incrs[b] = incr
 
         if b == 0:
             weights = (lax.dot_general(eye.astype(bf16), ygain, contract, preferred_element_type=f32)
                        * own_loc[0:1, :]).astype(bf16)
             qstate[...] = jnp.dot(weights, incr, preferred_element_type=f32)
-            for d in range(nz):
-                relay(1, d)
-            arrive(1)
-            for later in range(1, BATCHES):
-                unpack(later)
         else:
             q = qstate[...]
             xanom = (q - row_mean(q) + eye).astype(bf16)
             weights = (lax.dot_general(xanom, ygain, contract, preferred_element_type=f32)
                        * own_loc[b : b + 1, :]).astype(bf16)
             qstate[...] = q + jnp.dot(weights, incr, preferred_element_type=f32)
-
-        if b + 1 < BATCHES:
-            local = lxs[b]
-
-            @pl.loop(b + 1, BATCHES)
-            def _(later):
-                x = state[later]
-                xanom = (x - row_mean(x)).astype(bf16)
-                cov = lax.dot_general(xanom, ygain, contract, preferred_element_type=f32)
-                cov = cov.reshape(nz * nm, own, nobs) * local[:, None, :]
-                weights = cov.reshape(nobs, nobs).astype(bf16)
-                state[later] = x + jnp.dot(weights, incr, preferred_element_type=f32)
-
-        if 1 <= b <= nm - 1:
-            relay_ens(b - 1)
+        if b >= 4:
+            relay_ens(b - 3)
 
     q = qstate[...]
     q = (q - jnp.mean(q, axis=0, keepdims=True)).T.astype(bf16)
@@ -293,10 +334,9 @@
     qrecv[m] = qsend[pl.ds(base, rows), :]
     qcs = []
     for dm in range(1, nm):
-        to = pl.multiple_of(jnp.bitwise_xor(m, dm) * rows, rows)
+        to = place(jnp.bitwise_xor(m, dm))
         qcs.append(send(qsend.at[pl.ds(to, rows), :], qrecv.at[m], q_s.at[dm], q_r.at[dm], 0, dm))
     relay_ens(nm - 1)
-    keep.wait()
     for copy in qcs:
         copy.wait_recv()
     for kk in range(nm):
@@ -304,7 +344,7 @@
         edc[kk].wait_recv()
         part = slice(kk * block, (kk + 1) * block)
         delta = jnp.dot(qrecv[kk], every[:, part], preferred_element_type=f32)
-        out_ref[:, part] = (ens_ref[:, part].astype(f32) + delta).astype(bf16)
+        out_ref[:, part] = (every[pl.ds(base, rows), part].astype(f32) + delta).astype(bf16)
     for copy in sent:
         copy.wait_send()
 
@@ -314,38 +354,38 @@
     own = obs_site.shape[1]
     rows, width = ensemble.shape
     members, nobs, block = rows * nm, nz * nm * own, width // nm
-    loc = loc_pattern[:, 0, :].astype(jnp.float32)
-    head = jnp.concatenate([obs_value, obs_var, loc], axis=1)
-    head = jnp.pad(head, ((0, 0), (0, LANES - head.shape[1])))
-    sites = obs_site.astype(jnp.float32).reshape(-1)
-    sites = jnp.pad(sites, (0, 2 * LANES - sites.shape[0]), constant_values=-1.0)
-    meta = jnp.concatenate([head, sites.reshape(2, LANES)], axis=0)
     dma, bf16, f32 = pltpu.SemaphoreType.DMA, jnp.bfloat16, jnp.float32
-    two = [dma((2 * nz,))] * 2
+    two = [dma((3 * nz,))] * 2
     return pl.pallas_call(
         functools.partial(ensemble_kernel, nz, own),
         out_shape=jax.ShapeDtypeStruct(ensemble.shape, bf16),
-        in_specs=[pl.BlockSpec(memory_space=pltpu.VMEM)] * 2,
+        in_specs=[pl.BlockSpec(memory_space=pl.ANY)] * 5,
         out_specs=pl.BlockSpec(memory_space=pltpu.VMEM),
         scratch_shapes=[
             pltpu.VMEM((nz * nm, 8, LANES), f32),
             pltpu.VMEM((nz, members, BATCHES * LANES), bf16),
             pltpu.VMEM((members, width), bf16),
             pltpu.VMEM((BATCHES, nobs, members), f32),
+            pltpu.VMEM((BATCHES - 1, nobs, members), bf16),
+            pltpu.VMEM((BATCHES - 1, nobs, members), bf16),
             pltpu.VMEM((members, members), f32),
             pltpu.VMEM((2, nobs, 8), f32),
             pltpu.VMEM((BATCHES, nz * nm, nobs), f32),
             pltpu.VMEM((members, members), bf16),
             pltpu.VMEM((nm, rows, members), bf16),
+            pltpu.VMEM(obs_value.shape, f32),
+            pltpu.VMEM(obs_var.shape, f32),
+            pltpu.VMEM(obs_site.shape, jnp.int32),
+            pltpu.VMEM(loc_pattern.shape, jnp.int32),
             dma((nz * nm,)), dma((nz * nm,)),
-            *two, *two, *two, *two,
+            *two, *two, *two,
             *[dma((nm,))] * 8,
-            dma,
+            dma((5,)),
         ],
         compiler_params=pltpu.CompilerParams(
-            collective_id=0, has_side_effects=True, vmem_limit_bytes=48 * 2**20
+            collective_id=0, has_side_effects=True, vmem_limit_bytes=56 * 2**20
         ),
-    )(ensemble, meta)
+    )(ensemble, obs_value, obs_var, obs_site, loc_pattern)
 
 
 def dispatch(nz, nm, ensemble, obs_value, obs_var, obs_site, loc_pattern):

time: 55.1 us -> 53.2 us (0.966)
  local copies, waits for them, and re-layouts: 3.56 us -> 2.26 us
  other arithmetic: 0.78 us -> 0 us
    unnamed x9 -> x1, local copies, waits for them, and re-layouts: 3.47 us -> 2.26 us
    convert_element_type x2 -> x0, other arithmetic: 0.69 us -> none  [the longest x1 0.69 us: per_device_kernel(): sites = obs_site.astype(jnp.float32).reshape(-1)]
where the time goes in v2:
time: 53.2 us; the launch traced here: 53 us
  Pallas kernels  50.8 us (95%)
  local copies, waits for them, and re-layouts  2.26 us (4%)
    pallas_call x1, Pallas kernels, per_device_kernel(): pl.pallas_call(functools.partial(ensemble_kernel, nz, own), out_shape=jax...  50.8 us
    unnamed x1, local copies, waits for them, and re-layouts  2.26 us

profile of v2, /device:TPU:0, one launch (start us, length us, event | category | flops | bytes accessed | tf_op | source)
XLA Modules:
  0.0 53.0 jit_solution(1520052579928666399)
XLA Ops:
  0.0 50.8 %shard_map.55 = bf16[64,8192]{1,0:T(8,128)(2,1)} custom-call(bf16[64,8192]{1,0:T(8,128)(2,1)} %ens_ref.1, f32[6,32]{1,0:T(8,128)} %val_ref.1, f32[6,32]{1,0:T(8,128)} %var_ref.1, s32[6,32]{1,0:T(8,128)} %site_ref.1, s32[6,1,8]{2,1,0:T(1,128)} %loc_ref.1), custom_call_target="tpu_custom_call" | custom-call | tf_op jit(solution)/shard_map/pallas_call | solution.py:359
  50.8 2.3 %copy.7 = bf16[64,8192]{1,0:T(8,128)(2,1)} copy(bf16[64,8192]{1,0:T(8,128)(2,1)} %shard_map.55) | data formatting | bytes 2097152

commit v3 on v2

--- a/solution.py
+++ b/solution.py
@@ -234,9 +234,6 @@
     go_z(0, pair, 2 * rows)
     go_core(0, 0)
     go_z(1, base, rows)
-    xc[2, 0].wait_recv()
-    go_z(2, pair, 2 * rows)
-    go_core(2, 0)
 
     for dz, dm in others:
         if dz:
@@ -262,6 +259,9 @@
     for d in range(1, nz):
         zc[1, d].wait_recv()
         go_x(1, d)
+    xc[2, 0].wait_recv()
+    go_z(2, pair, 2 * rows)
+    go_core(2, 0)
     for kk in range(1, nm):
         send_ens(kk)
 

time: 53.2 us -> 49 us (0.921)
  Pallas kernels: 50.8 us -> 46.5 us
    pallas_call x1, Pallas kernels: 50.8 us -> 46.5 us  [per_device_kernel(): pl.pallas_call(functools.partial(ensemble_kernel, nz, own), out_shape=jax...]
where the time goes in v3:
time: 49 us; the launch traced here: 48.8 us
  Pallas kernels  46.5 us (95%)
  local copies, waits for them, and re-layouts  2.26 us (5%)
    pallas_call x1, Pallas kernels, per_device_kernel(): pl.pallas_call(functools.partial(ensemble_kernel, nz, own), out_shape=jax...  46.5 us
    unnamed x1, local copies, waits for them, and re-layouts  2.26 us

profile of v3, /device:TPU:0, one launch (start us, length us, event | category | flops | bytes accessed | tf_op | source)
XLA Modules:
  0.0 48.8 jit_solution(17670182708477901435)
XLA Ops:
  0.0 46.5 %shard_map.55 = bf16[64,8192]{1,0:T(8,128)(2,1)} custom-call(bf16[64,8192]{1,0:T(8,128)(2,1)} %ens_ref.1, f32[6,32]{1,0:T(8,128)} %val_ref.1, f32[6,32]{1,0:T(8,128)} %var_ref.1, s32[6,32]{1,0:T(8,128)} %site_ref.1, s32[6,1,8]{2,1,0:T(1,128)} %loc_ref.1), custom_call_target="tpu_custom_call" | custom-call | tf_op jit(solution)/shard_map/pallas_call | solution.py:359
  46.5 2.3 %copy.7 = bf16[64,8192]{1,0:T(8,128)(2,1)} copy(bf16[64,8192]{1,0:T(8,128)(2,1)} %shard_map.55) | data formatting | bytes 2097152

commit v4 on v3

--- a/solution.py
+++ b/solution.py
@@ -200,7 +200,7 @@
     cols[z, pl.ds(base, rows), 0 : nm * LANES] = placed
     cols[z, pl.ds(base, rows), nm * LANES : BATCHES * LANES] = placed2
 
-    chunks = ((0, 1), (1, 3), (3, BATCHES))
+    chunks = ((0, 1), (1, 3), (3, 4), (4, BATCHES))
 
     def view(d, c, start, count):
         low, high = chunks[c]
@@ -229,6 +229,7 @@
 
     go_x(0, 0)
     go_x(2, 0)
+    go_x(3, 0)
     go_x(1, 0)
     xc[0, 0].wait_recv()
     go_z(0, pair, 2 * rows)
@@ -259,9 +260,10 @@
     for d in range(1, nz):
         zc[1, d].wait_recv()
         go_x(1, d)
-    xc[2, 0].wait_recv()
-    go_z(2, pair, 2 * rows)
-    go_core(2, 0)
+    for c in (2, 3):
+        xc[c, 0].wait_recv()
+        go_z(c, pair, 2 * rows)
+        go_core(c, 0)
     for kk in range(1, nm):
         send_ens(kk)
 
@@ -282,10 +284,11 @@
                     for d in range(nz):
                         xc[1, d].wait_recv()
                         go_core(1, d)
+                if c >= 2:
+                    for d in range(1, nz):
+                        zc[c, d].wait_recv()
+                        go_core(c, d)
                 if c == 2:
-                    for d in range(1, nz):
-                        zc[2, d].wait_recv()
-                        go_core(2, d)
                     relay_ens(0)
                 arrive(c)
                 for fresh in range(low, high):
@@ -355,7 +358,7 @@
     rows, width = ensemble.shape
     members, nobs, block = rows * nm, nz * nm * own, width // nm
     dma, bf16, f32 = pltpu.SemaphoreType.DMA, jnp.bfloat16, jnp.float32
-    two = [dma((3 * nz,))] * 2
+    two = [dma((4 * nz,))] * 2
     return pl.pallas_call(
         functools.partial(ensemble_kernel, nz, own),
         out_shape=jax.ShapeDtypeStruct(ensemble.shape, bf16),

time: 49 us -> 50.2 us (1.024)
  Pallas kernels: 46.5 us -> 47.7 us
    pallas_call x1, Pallas kernels: 46.5 us -> 47.7 us  [per_device_kernel(): pl.pallas_call(functools.partial(ensemble_kernel, nz, own), out_shape=jax...]
where the time goes in v4:
time: 50.2 us; the launch traced here: 50 us
  Pallas kernels  47.7 us (95%)
  local copies, waits for them, and re-layouts  2.26 us (5%)
    pallas_call x1, Pallas kernels, per_device_kernel(): pl.pallas_call(functools.partial(ensemble_kernel, nz, own), out_shape=jax...  47.7 us
    unnamed x1, local copies, waits for them, and re-layouts  2.26 us

profile of v4, /device:TPU:0, one launch (start us, length us, event | category | flops | bytes accessed | tf_op | source)
XLA Modules:
  0.0 50.0 jit_solution(3367672872045155797)
XLA Ops:
  0.0 47.7 %shard_map.55 = bf16[64,8192]{1,0:T(8,128)(2,1)} custom-call(bf16[64,8192]{1,0:T(8,128)(2,1)} %ens_ref.1, f32[6,32]{1,0:T(8,128)} %val_ref.1, f32[6,32]{1,0:T(8,128)} %var_ref.1, s32[6,32]{1,0:T(8,128)} %site_ref.1, s32[6,1,8]{2,1,0:T(1,128)} %loc_ref.1), custom_call_target="tpu_custom_call" | custom-call | tf_op jit(solution)/shard_map/pallas_call | solution.py:362
  47.7 2.3 %copy.7 = bf16[64,8192]{1,0:T(8,128)(2,1)} copy(bf16[64,8192]{1,0:T(8,128)(2,1)} %shard_map.55) | data formatting | bytes 2097152
